TPU v7x, 256 devices: a whole 4x4x8 slice. The times are simulated.
256 devices in a mesh: queue: 32 (over z, y_hi, core), tp: 8 (over y_lo, x).
Axes of the slice: x: 4, y: 4 (y_hi: 2, y_lo: 2; y = y_hi * 2 + y_lo), z: 8, core: 2. Of those that a mesh axis runs over, the one named last changes fastest.
Arguments:
- latents: bfloat16 [12288, 3072], P('queue'), may hold values from -6 to 6
- fresh_noise: bfloat16 [192, 3072], P(None, 'tp'), may hold values from -6 to 6
- levels: int32 [32], P('queue'), may hold values from 0 to 49, as said below
- frame_counts: int32 [32], P('queue'), may hold values from 1 to 2, as said below
- modulation: float32 [50, 2, 3072], replicated, may hold values from -2.5 to 2.5
- w_qkv: bfloat16 [3072, 3, 3072], P(None, None, 'tp')
- w_out: bfloat16 [3072, 3072], P('tp'), may hold values from -0.109375 to 0.109375
- sampler_coef: float32 [2, 50], replicated, may hold values from -1.2 to 1.2
Outputs:
- queue_next: bfloat16 [12288, 3072], P('queue', 'tp')
- finished: bfloat16 [192, 3072], P('queue', 'tp')
Inputs may be any that keep to these rules, and one draw needn't show every extreme that they name: `levels`: levels rise along the queue: group c has a level within one of c * 49 // 31; the first group has 0 and the last 49. `frame_counts`: the first 2 - count frame slots of a group are empty; some group is full and some group has one frame.
All inputs are finite; a program needn't handle non-finite values.
Results may differ from a plain program's by a relative error of at most 0.0075.
The roundings to bfloat16 on the way count: a program that leaves them out, or rounds other values in their place, can miss the bound.
Values may be sent and summed in bfloat16 or wider, within the bound.
A program may use at most 64 MiB of HBM per device.

v0:
```python
import jax
import jax.numpy as jnp
from jax import lax
from jax.sharding import PartitionSpec as P

HEAD_DIM = 64
FRAMES = 2
FRAME_TOK = 192


def passed_along(value, axis, steps):
    count = lax.axis_size(axis)
    initial, last = (max(0, -steps), min(count, count - steps))
    return lax.ppermute(value, axis, [(source, source + steps) for source in range(initial, last)])


def from_root(block, axis, owner):
    block = jnp.where(lax.axis_index(axis) == owner, block, jnp.zeros_like(block))
    return lax.psum(block, axis)


def body(latents, fresh_noise, levels, frame_counts, modulation, w_qkv, w_out, sampler_coef):
    queue_size = lax.axis_size("queue")
    tp_rank = lax.axis_index("tp")
    queue_rank = lax.axis_index("queue")
    rows = latents.shape[0]
    local = w_out.shape[0]
    heads_here = local // HEAD_DIM
    level = levels[0]
    count = frame_counts[0]
    table = modulation[level]
    rows_float = latents.astype(jnp.float32)
    center = jnp.mean(rows_float, axis=1, keepdims=True)
    spread = jnp.mean((rows_float - center) ** 2, axis=1, keepdims=True)
    normed = (rows_float - center) * lax.rsqrt(spread + 1e-06)
    normed = (normed * (1.0 + table[1][None, :]) + table[0][None, :]).astype(jnp.bfloat16)
    weight_flat = w_qkv.reshape(w_qkv.shape[0], 3 * local)
    projected = jnp.dot(normed, weight_flat, preferred_element_type=jnp.float32).astype(
        jnp.bfloat16
    )
    own = projected.reshape(rows, 3, heads_here, HEAD_DIM)
    outgoing = projected[rows - FRAME_TOK :, local:].reshape(FRAME_TOK, 2, local)
    prior = passed_along(outgoing, "queue", 1).reshape(FRAME_TOK, 2, heads_here, HEAD_DIM)
    queries = own[:, 0]
    key_set = jnp.concatenate([prior[:, 0], own[:, 1]], axis=0)
    val_set = jnp.concatenate([prior[:, 1], own[:, 2]], axis=0)
    scores = jnp.einsum("qhd,khd->hqk", queries, key_set, preferred_element_type=jnp.float32)
    scores = scores * (1.0 / float(HEAD_DIM) ** 0.5)
    position = jnp.arange(FRAME_TOK + rows, dtype=jnp.int32)
    own_frame = (position - FRAME_TOK) // FRAME_TOK
    live = jnp.where(position < FRAME_TOK, queue_rank > 0, own_frame >= FRAMES - count)
    masked = jnp.where(live[None, None, :], scores, jnp.float32(-1e30))
    top = jnp.max(masked, axis=2, keepdims=True)
    expo = jnp.exp(masked - top)
    weights = (expo / jnp.sum(expo, axis=2, keepdims=True)).astype(jnp.bfloat16)
    attended = jnp.einsum("hqk,khd->qhd", weights, val_set, preferred_element_type=jnp.float32)
    attended = attended.astype(jnp.bfloat16).reshape(rows, local)
    partial_out = jnp.dot(attended, w_out, preferred_element_type=jnp.float32)
    summed = lax.psum(partial_out, "tp")
    branch = lax.dynamic_slice_in_dim(summed, tp_rank * local, local, 1)
    current = lax.dynamic_slice_in_dim(latents, tp_rank * local, local, 1).astype(jnp.float32)
    updated = sampler_coef[0, level] * current + sampler_coef[1, level] * (current + branch)
    row_frame = jnp.arange(rows, dtype=jnp.int32) // FRAME_TOK
    valid = row_frame >= FRAMES - count
    updated = jnp.where(valid[:, None], updated, current)
    rounded = updated.astype(jnp.bfloat16)
    leading = rounded[:FRAME_TOK]
    arriving = passed_along(leading, "queue", -1)
    arriving = jnp.where(queue_rank == queue_size - 1, fresh_noise, arriving)
    queue_next = jnp.concatenate([rounded[FRAME_TOK:], arriving], axis=0)
    whole_frame = from_root(leading, "queue", 0)
    share_rows = FRAME_TOK // queue_size
    finished = lax.dynamic_slice_in_dim(whole_frame, queue_rank * share_rows, share_rows, 0)
    return (queue_next, finished)


def solution(mesh):
    placed = (
        P("queue", None),
        P(None, "tp"),
        P("queue"),
        P("queue"),
        P(),
        P(None, None, "tp"),
        P("tp", None),
        P(),
    )
    return jax.shard_map(
        body,
        mesh=mesh,
        in_specs=placed,
        out_specs=(P("queue", "tp"), P("queue", "tp")),
        check_vma=False,
    )
```

profile of v0, /device:TPU:1, one launch (start us, length us, event | category | flops | bytes accessed | tf_op | source)
XLA Modules:
  0.0 443.3 jit_solution(10674793835158231514)
XLA Ops:
  8.0 2.1 convert_reduce_fusion
  10.1 2.4 fusion.3
  12.5 10.3 %copy.14 = bf16[3072,3,384]{0,2,1:T(8,128)(2,1)} copy(bf16[3072,3,384]{2,0,1:T(8,128)(2,1)} %param.13) | data formatting | bytes 14155776 | tf_op args[5]
  22.8 0.8 dynamic-slice_add_fusion
  23.6 7.2 %convolution_convert_fusion = bf16[384,1152]{1,0:T(8,128)(2,1)S(1)} fusion(bf16[3072,1152]{0,1:T(8,128)(2,1)} %bitcast.36, bf16[384,3072]{1,0:T(8,128)(2,1)} %param.8, f32[3072]{0:T(1024)S(1)} %bitcast.42, f32[3072]{0:T(1024)S(1)} %bitcast.41, f32[384]{0:T(512)S(1)} %add_rsqrt_fusion, f32[384]{0:T(512)S(1)} %broadcast_multiply_fusion), kind=kOutput, calls=%fused_computation.13 | convolution fusion | flops 2725429248 | bytes 10349568 | tf_op jit(solution)/shard_map/dot_general | solution.py:38
  30.9 0.9 copy-done.1
  31.9 6.2 %collective-permute-start = (bf16[192,2,384]{2,1,0:T(2,128)(2,1)S(1)}, bf16[192,2,384]{2,1,0:T(2,128)(2,1)}, u32[]{:S(2)}, u32[]{:S(2)}) collective-permute-start(bf16[192,2,384]{2,1,0:T(2,128)(2,1)S(1)} %reshape.78), channel_id=1, source_target_pairs={{0,8},{8,16},{16,24},{24,32},{32,40},{40,48},{48,56},{56,64},{64,7... | collective-permute-start | bytes 884744 | tf_op jit(solution)/shard_map/ppermute | solution.py:14
  38.8 1.8 copy.16
  40.6 0.9 slice_bitcast_fusion.2
  41.4 0.3 collective-permute-done
  41.8 1.9 copy.15
  43.7 1.8 slice_bitcast_fusion.8
  45.5 5.5 %fusion.41 = (f32[6,384]{1,0:T(8,128)S(1)}, f32[6,384,576]{1,2,0:T(8,128)}) fusion(pred[576]{0:T(1024)(128)(4,1)S(1)} %fusion.28, bf16[384,6,64]{0,2,1:T(8,128)(2,1)} %get-tuple-element.5, bf16[192,6,64]{0,2,1:T(8,128)(2,1)} %get-tuple-element.7, bf16[384,3,6,64]{0,3,2,1:T(8,128)(2,1)S(1)} %bitcast.38), kind=kOutput, calls=%fused_computation.71 | convolution fusion | flops 176063040 | bytes 6055936 | tf_op jit(solution)/shard_map/sub | solution.py:54
  51.0 3.3 fusion.17
  54.4 3.6 fusion.42
  58.1 0.7 constant_dynamic-slice_fusion.2
  58.7 123.8 %all-reduce.3.cloned.1.call-done = f32[384,3072]{1,0:T(8,128)} async-done(((f32[384,3072]{1,0:T(8,128)}), f32[384,3072]{1,0:T(8,128)}) %all-reduce.3.cloned.1.call-update) | async-done | bytes 4718608 | tf_op jit(solution)/shard_map/psum | solution.py:59
  182.5 2.6 fusion.20
  185.1 0.7 broadcast_select_fusion
  185.8 2.6 collective-permute-start.1
  188.4 5.3 %collective-permute-done.1 = bf16[192,384]{1,0:T(8,128)(2,1)S(1)} collective-permute-done((bf16[192,384]{1,0:T(8,128)(2,1)S(1)}, bf16[192,384]{1,0:T(8,128)(2,1)S(1)}, u32[]{:S(2)}, u32[]{:S(2)}) %collective-permute-start.1) | collective-permute-done | bytes 147488 | tf_op jit(solution)/shard_map/ppermute | solution.py:14
  193.7 0.7 pad_maximum_fusion.7
  194.5 240.7 %all-reduce.5.cloned.1.call-done = bf16[192,384]{1,0:T(8,128)(2,1)} async-done(((bf16[192,384]{1,0:T(8,128)(2,1)}), bf16[192,384]{1,0:T(8,128)(2,1)}) %all-reduce.5.cloned.1.call-update) | async-done | bytes 147472 | tf_op jit(solution)/shard_map/psum | solution.py:19
  435.2 1.3 constant_dynamic-slice_fusion
  (20 shorter events, 0.3 us)
Async XLA Ops:
  7.2 47.2 %copy-start = (bf16[384,3072]{1,0:T(8,128)(2,1)S(1)}, bf16[384,3072]{1,0:T(8,128)(2,1)}, u32[]{:S(2)}) copy-start(bf16[384,3072]{1,0:T(8,128)(2,1)} %param.14) | copy-start | bytes 7077892
  7.2 175.3 %all-reduce.3.cloned.1.call-start = ((), (), s32[]{:S(2)}) async-start(), calls=%async_computation | async-start | bytes 9437184 | tf_op jit(solution)/shard_map/psum | solution.py:59
  30.9 0.9 copy-start.1
  31.9 9.9 %collective-permute-start = (bf16[192,2,384]{2,1,0:T(2,128)(2,1)S(1)}, bf16[192,2,384]{2,1,0:T(2,128)(2,1)}, u32[]{:S(2)}, u32[]{:S(2)}) collective-permute-start(bf16[192,2,384]{2,1,0:T(2,128)(2,1)S(1)} %reshape.78), channel_id=1, source_target_pairs={{0,8},{8,16},{16,24},{24,32},{32,40},{40,48},{48,56},{56,64},{64,7... | collective-permute-start | bytes 884744 | tf_op jit(solution)/shard_map/ppermute | solution.py:14
  45.5 5.5 %copy-start.2 = (bf16[384,6,64]{0,2,1:T(8,128)(2,1)S(1)}, bf16[384,6,64]{0,2,1:T(8,128)(2,1)}, u32[]{:S(2)}) copy-start(bf16[384,6,64]{0,2,1:T(8,128)(2,1)} %get-tuple-element.4) | copy-start | bytes 884740
  54.4 3.7 copy-start.4
  58.0 135.8 %copy-start.3 = (bf16[192,384]{1,0:T(8,128)(2,1)S(1)}, bf16[192,384]{1,0:T(8,128)(2,1)}, u32[]{:S(2)}) copy-start(bf16[192,384]{1,0:T(8,128)(2,1)} %param.9) | copy-start | bytes 442372
  58.0 377.2 %all-reduce.5.cloned.1.call-start = ((), (), s32[]{:S(2)}) async-start(), calls=%async_computation.1 | async-start | bytes 294912 | tf_op jit(solution)/shard_map/psum | solution.py:19
  185.8 8.0 %collective-permute-start.1 = (bf16[192,384]{1,0:T(8,128)(2,1)S(1)}, bf16[192,384]{1,0:T(8,128)(2,1)S(1)}, u32[]{:S(2)}, u32[]{:S(2)}) collective-permute-start(bf16[192,384]{1,0:T(8,128)(2,1)S(1)} %get-tuple-element.9), channel_id=1, source_target_pairs={{8,0},{16,8},{24,16},{32,24},{40,32},{48,40},{56,48},{64,56},{72,6... | collective-permute-start | bytes 442376 | tf_op jit(solution)/shard_map/ppermute | solution.py:14
Sparse Core Ops, SparseCore 0:
  58.1 124.3 all-reduce.2
  188.5 246.6 all-reduce.4
where the time goes:
time: 444 us; the launch traced here: 443 us
  waiting for transfers between devices  370 us (83%)
  matrix products  19.7 us (4%)
  local copies, waits for them, and re-layouts  19.6 us (4%)
  between operations  15.6 us (4%)
  other arithmetic  9.38 us (2%)
  starting transfers between devices  8.86 us (2%)
    psum x1, waiting for transfers between devices, from_root(): return lax.psum(block, axis)  241 us
    psum x1, waiting for transfers between devices, body(): summed = lax.psum(partial_out, 'tp')  124 us
    unnamed x11, local copies, waits for them, and re-layouts  11.2 us
  transfers between devices with their start and end apart: 4, of which 4 were waited for; matrix products, arithmetic and copies ran while one was open for 1% of the time, Pallas kernels for 0%

commit v1 on v0

v1 whole, which is shorter than its diff:
```python
import jax
import jax.numpy as jnp
from jax import lax
from jax.experimental import pallas as pl
from jax.experimental.pallas import tpu as pltpu
from jax.sharding import PartitionSpec as P

MESH = pl.DeviceIdType.MESH
BF = jnp.bfloat16
F32 = jnp.float32
D = 3072
W = 384
ROWS = 384
TOK = 192
NX = 4
C = 128
NC = 3
BIG = 1e30


def kernel(
    nq, levels, counts, coef, lat_hbm, mod_hbm, wqkv_hbm, wout_hbm, fresh_hbm,
    out_ref, fin_ref,
    lat, mod, wbuf, normed, qbuf, kown, vt, kpri, vpri, vtp, wo, fw, ag,
    acc, rsend, rrecv, f0, f0f, arr, finsrc, findst,
    ld_sem, kv_s, kv_r, wo_s, wo_r, ag_s, ag_r, rs_s, rs_r, f_s, f_r, fin_s, fin_r, fresh_sem,
):
    q = lax.axis_index("queue")
    t = lax.axis_index("tp")
    x = lax.rem(t, NX)
    y = t // NX
    xr, xl, xo = lax.rem(x + 1, NX), lax.rem(x + 3, NX), lax.rem(x + 2, NX)
    right, left = y * NX + xr, y * NX + xl
    ypeer = (1 - y) * NX + x
    core = lax.rem(q, 2)
    sib = q + 1 - 2 * core

    def load(src, dst, i):
        return pltpu.make_async_copy(src, dst, ld_sem.at[i])

    def remote(src, dst, ss, rs, **dev):
        return pltpu.make_async_remote_copy(
            src_ref=src, dst_ref=dst, send_sem=ss, recv_sem=rs, device_id=dev, device_id_type=MESH
        )

    ld_f1 = load(lat_hbm.at[pl.ds(TOK, TOK)], lat.at[pl.ds(TOK, TOK)], 0)
    ld_mod = load(mod_hbm, mod, 1)
    ld_k = load(wqkv_hbm.at[1], wbuf.at[:, pl.ds(0, W)], 2)
    ld_v = load(wqkv_hbm.at[2], wbuf.at[:, pl.ds(W, W)], 3)
    ld_f0 = load(lat_hbm.at[pl.ds(0, TOK)], lat.at[pl.ds(0, TOK)], 4)
    ld_q = load(wqkv_hbm.at[0], wbuf.at[:, pl.ds(2 * W, W)], 5)

    def col(block):
        return pl.ds(pl.multiple_of(block * W, 128), W)

    ld_o = [load(wout_hbm.at[:, col(j * NX + x)], wo.at[j, pl.ds(0, W)], 6 + j) for j in range(2)]
    for c in (ld_f1, ld_mod, ld_k, ld_v, ld_f0, ld_q, *ld_o):
        c.start()

    barrier = pltpu.get_barrier_semaphore()
    for dev in ({"tp": right}, {"tp": left}, {"tp": ypeer}):
        pl.semaphore_signal(barrier, inc=1, device_id=dev, device_id_type=MESH)

    @pl.when(q > 0)
    def _():
        pl.semaphore_signal(barrier, inc=1, device_id={"queue": q - 1}, device_id_type=MESH)

    @pl.when(q < nq - 1)
    def _():
        pl.semaphore_signal(barrier, inc=1, device_id={"queue": q + 1}, device_id_type=MESH)

    @pl.when(q > 1)
    def _():
        pl.semaphore_signal(barrier, inc=1, device_id={"queue": 0}, device_id_type=MESH)

    @pl.when(q == 0)
    def _():
        pl.semaphore_wait(barrier, 4 + nq - 2)

    @pl.when((q > 0) & (q < nq - 1))
    def _():
        pl.semaphore_wait(barrier, 5)

    @pl.when(q == nq - 1)
    def _():
        pl.semaphore_wait(barrier, 4)

    wc = wo.at[core]
    H = W // 2
    opp = col(core * NX + xo)
    wo_via_r = remote(wout_hbm.at[pl.ds(0, H), opp], fw.at[0], wo_s.at[2], wo_r.at[2], tp=right)
    wo_via_l = remote(wout_hbm.at[pl.ds(H, H), opp], fw.at[1], wo_s.at[3], wo_r.at[3], tp=left)
    wo_r1 = remote(wout_hbm.at[:, col(core * NX + xr)], wc.at[pl.ds(W, W)], wo_s.at[0], wo_r.at[0], tp=right)
    wo_l1 = remote(wout_hbm.at[:, col(core * NX + xl)], wc.at[pl.ds(3 * W, W)], wo_s.at[1], wo_r.at[1], tp=left)
    wo_fr = remote(fw.at[0], wc.at[pl.ds(2 * W, H)], wo_s.at[4], wo_r.at[4], tp=right)
    wo_fl = remote(fw.at[1], wc.at[pl.ds(2 * W + H, H)], wo_s.at[5], wo_r.at[5], tp=left)
    wo_sib = [
        remote(wc.at[pl.ds(s * W, W)], wc.at[pl.ds(s * W, W)], wo_s.at[5 + s], wo_r.at[5 + s], queue=sib)
        for s in (1, 2, 3)
    ]
    for c in (wo_via_r, wo_via_l, wo_r1, wo_l1):
        c.start()

    level = levels[0]
    count = counts[0]
    full = count == 2
    c_lat = coef[0, level]
    c_out = coef[1, level]

    def norm(start):
        table = mod[level]
        gain = 1.0 + table[1:2]
        shift = table[0:1]

        def step(i, _):
            rows = pl.ds(pl.multiple_of(start + i * 16, 16), 16)
            v = lat[rows, :].astype(F32)
            d = v - jnp.mean(v, axis=1, keepdims=True)
            s = jnp.mean(d * d, axis=1, keepdims=True)
            normed[rows, :] = (d * lax.rsqrt(s + 1e-6) * gain + shift).astype(BF)
            return 0

        lax.fori_loop(0, TOK // 16, step, 0, unroll=2)

    def mm(start, rows, lo, width):
        return jnp.dot(
            normed[pl.ds(start, rows), :], wbuf[:, pl.ds(lo, width)], preferred_element_type=F32
        ).astype(BF)

    kv_k = remote(kown.at[pl.ds(TOK, TOK)], kpri, kv_s.at[0], kv_r.at[0], queue=q + 1)
    kv_v = remote(f0.at[1], vpri, kv_s.at[1], kv_r.at[1], queue=q + 1)

    ld_f1.wait()
    ld_mod.wait()
    norm(TOK)
    ld_k.wait()
    ld_v.wait()
    kown[pl.ds(TOK, TOK), pl.ds(0, 256)] = mm(TOK, TOK, 0, 256)
    mid = mm(TOK, TOK, 256, 256)
    kown[pl.ds(TOK, TOK), pl.ds(256, 128)] = mid[:, :128]

    @pl.when(q < nq - 1)
    def _():
        kv_k.start()

    f0[1, :, pl.ds(0, 128)] = mid[:, 128:]
    f0[1, :, pl.ds(128, 256)] = mm(TOK, TOK, 512, 256)

    @pl.when(q < nq - 1)
    def _():
        kv_v.start()

    @pl.when(q == 0)
    def _():
        kpri[...] = jnp.zeros_like(kpri)
        vpri[...] = jnp.zeros_like(vpri)

    ld_f0.wait()
    norm(0)

    wo_via_r.wait_recv()
    wo_fr.start()
    wo_via_l.wait_recv()
    wo_fl.start()

    ld_q.wait()
    qbuf[:, pl.ds(0, 256)] = mm(0, ROWS, 2 * W, 256) * BF(0.125)
    qbuf[:, pl.ds(256, 128)] = mm(0, ROWS, 2 * W + 256, 128) * BF(0.125)
    kown[pl.ds(0, TOK), pl.ds(0, 256)] = mm(0, TOK, 0, 256)
    mid = mm(0, TOK, 256, 256)
    kown[pl.ds(0, TOK), pl.ds(256, 128)] = mid[:, :128]
    v0 = jnp.concatenate([mid[:, 128:], mm(0, TOK, 512, 256)], axis=1)
    vt[...] = jnp.concatenate([v0, f0[1]], axis=0).T

    lane = lax.broadcasted_iota(jnp.int32, (C, C), 1)
    row = lax.broadcasted_iota(jnp.int32, (C, C), 0)
    has_prior = q > 0
    even = (lane < 64).astype(F32)
    odd = 1.0 - even

    def att_pair(r, p):
        lanes = pl.ds(p * 128, 128)
        qp = qbuf[pl.ds(r * C, C), lanes].astype(F32)
        qs = jnp.concatenate([qp * even, qp * odd], axis=0).astype(BF)
        nt = (((1,), (1,)), ((), ()))
        so = lax.dot_general(kown[:, lanes], qs, nt, preferred_element_type=F32)
        sp = lax.dot_general(kpri[:, lanes], qs, nt, preferred_element_type=F32)
        s0, s1 = so[:TOK], so[TOK:]
        m0 = jnp.where(full, jnp.max(s0, axis=0, keepdims=True), -BIG)
        m1 = jnp.max(s1, axis=0, keepdims=True)
        mp = jnp.where(has_prior, jnp.max(sp, axis=0, keepdims=True), -BIG)
        top = jnp.maximum(jnp.maximum(m0, m1), mp)
        e0 = jnp.exp(s0 - jnp.where(full, top, BIG))
        e1 = jnp.exp(s1 - top)
        ep = jnp.exp(sp - jnp.where(has_prior, top, BIG))
        total = (
            jnp.sum(e0, axis=0, keepdims=True)
            + jnp.sum(e1, axis=0, keepdims=True)
            + jnp.sum(ep, axis=0, keepdims=True)
        )
        inv = 1.0 / total
        w_own = jnp.concatenate([(e0 * inv).astype(BF), (e1 * inv).astype(BF)], axis=0)
        w_pri = (ep * inv).astype(BF)
        o = jnp.dot(vt[lanes, :], w_own, preferred_element_type=F32)
        o = o + jnp.dot(vtp[lanes, :], w_pri, preferred_element_type=F32)
        ot = jnp.where(row < 64, o[:, :C], o[:, C:])
        ag[r, :, lanes] = ot.T.astype(BF)

    ag_dir, ag_fwd = [], []
    for r in range(NC):
        own = ag.at[r, :, pl.ds(0, W)]
        ag_dir.append((
            remote(own, ag.at[r, :, pl.ds(W, W)], ag_s.at[r, 0], ag_r.at[r, 0], tp=right),
            remote(own, ag.at[r, :, pl.ds(3 * W, W)], ag_s.at[r, 1], ag_r.at[r, 1], tp=left),
        ))
        top_half, low_half = pl.ds(0, C // 2), pl.ds(C // 2, C // 2)
        ag_fwd.append((
            remote(ag.at[r, top_half, pl.ds(W, W)], ag.at[r, top_half, pl.ds(2 * W, W)],
                   ag_s.at[r, 2], ag_r.at[r, 2], tp=right),
            remote(ag.at[r, low_half, pl.ds(3 * W, W)], ag.at[r, low_half, pl.ds(2 * W, W)],
                   ag_s.at[r, 3], ag_r.at[r, 3], tp=left),
        ))

    def ag_start(r):
        for c in ag_dir[r]:
            c.start()

    def ag_forward(r):
        for got, on in zip(ag_dir[r], ag_fwd[r]):
            got.wait_recv()
            on.start()

    rs = [remote(rsend.at[r], rrecv.at[r], rs_s.at[r], rs_r.at[r], tp=ypeer) for r in range(NC)]

    def proj(r):
        for c in ag_fwd[r]:
            c.wait_recv()
        a = ag[r]
        rsend[r] = jnp.dot(a, wo[1 - y], preferred_element_type=F32).astype(BF)
        rs[r].start()
        acc[r] = jnp.dot(a, wo[y], preferred_element_type=F32)

    def final(r):
        rs[r].wait_recv()
        branch = acc[r] + rrecv[r].astype(F32)
        cur = lat[pl.ds(r * C, C), col(t)].astype(F32)
        upd = c_lat * cur + c_out * (cur + branch)
        if r == 0:
            valid = full
        elif r == 2:
            valid = True
        else:
            valid = full | (lax.broadcasted_iota(jnp.int32, (C, W), 0) >= TOK - C)
        if valid is not True:
            upd = jnp.where(valid, upd, cur)
        return upd

    @pl.when(q > 0)
    def _():
        kv_k.wait_recv()
        kv_v.wait_recv()

    vtp[...] = vpri[...].T

    for p in range(3):
        att_pair(0, p)
    ag_start(0)
    wo_r1.wait_recv()
    wo_sib[0].start()
    for p in range(3):
        att_pair(1, p)
        if p == 0:
            ag_forward(0)
    ag_start(1)
    wo_l1.wait_recv()
    wo_sib[2].start()
    wo_fr.wait_recv()
    wo_fl.wait_recv()
    wo_sib[1].start()
    att_pair(2, 0)
    ag_forward(1)
    for c in ld_o:
        c.wait()
    for c in wo_sib:
        c.wait_recv()
    proj(0)
    att_pair(2, 1)
    att_pair(2, 2)
    ag_start(2)
    proj(1)
    ag_forward(2)

    f_a = remote(f0.at[0, pl.ds(0, C)], arr.at[pl.ds(0, C)], f_s.at[0], f_r.at[0], queue=q - 1)
    f_b = remote(
        f0.at[0, pl.ds(C, TOK - C)], arr.at[pl.ds(C, TOK - C)], f_s.at[1], f_r.at[1], queue=q - 1
    )
    fresh = pltpu.make_async_copy(fresh_hbm, arr, fresh_sem)

    @pl.when(q == nq - 1)
    def _():
        fresh.start()

    u = final(0)
    f0[0, pl.ds(0, C)] = u.astype(BF)
    f0f[pl.ds(0, C)] = u

    @pl.when(q > 0)
    def _():
        f_a.start()

    proj(2)
    u = final(1)
    f0[0, pl.ds(C, TOK - C)] = u[: TOK - C].astype(BF)
    f0f[pl.ds(C, TOK - C)] = u[: TOK - C]
    out_ref[pl.ds(0, 2 * C - TOK)] = u[TOK - C :].astype(BF)

    @pl.when(q > 0)
    def _():
        f_b.start()

    share = TOK // nq

    def fin_copy(i):
        return remote(finsrc.at[i], findst, fin_s.at[i], fin_r.at[0], queue=i)

    @pl.when(q == 0)
    def _():
        f0f[pl.ds(TOK, 16)] = jnp.zeros((16, W), F32)
        for i in range(nq):
            finsrc[i] = f0f[pl.ds(i * share, 16)].astype(BF)

        def go(i, _):
            fin_copy(i).start()
            return 0

        lax.fori_loop(1, nq, go, 0)

    out_ref[pl.ds(2 * C - TOK, C)] = final(2).astype(BF)

    @pl.when(q > 0)
    def _():
        f_a.wait_send()
        f_b.wait_send()
        fin_copy(0).wait_recv()
        fin_ref[...] = findst[pl.ds(0, share)]

    @pl.when(q == 0)
    def _():
        fin_ref[...] = finsrc[0, pl.ds(0, share)]

        def done(i, _):
            fin_copy(i).wait_send()
            return 0

        lax.fori_loop(1, nq, done, 0)

    @pl.when(q < nq - 1)
    def _():
        kv_k.wait_send()
        kv_v.wait_send()
        f_a.wait_recv()
        f_b.wait_recv()

    @pl.when(q == nq - 1)
    def _():
        fresh.wait()

    out_ref[pl.ds(TOK, TOK)] = arr[...]
    for c in (wo_via_r, wo_via_l, wo_r1, wo_l1, wo_fr, wo_fl, *wo_sib, *rs):
        c.wait_send()
    for r in range(NC):
        for c in (*ag_dir[r], *ag_fwd[r]):
            c.wait_send()


def solution(mesh):
    nq = mesh.shape["queue"]

    def step(latents, fresh_noise, levels, frame_counts, modulation, w_qkv, w_out, sampler_coef):
        anyspace = pl.BlockSpec(memory_space=pl.ANY)
        smem = pl.BlockSpec(memory_space=pltpu.SMEM)
        vmem = pl.BlockSpec(memory_space=pltpu.VMEM)
        dma = pltpu.SemaphoreType.DMA
        return pl.pallas_call(
            lambda *refs: kernel(nq, *refs),
            out_shape=(
                jax.ShapeDtypeStruct((ROWS, W), BF),
                jax.ShapeDtypeStruct((TOK // nq, W), BF),
            ),
            in_specs=[smem, smem, smem] + [anyspace] * 5,
            out_specs=(vmem, vmem),
            scratch_shapes=[
                pltpu.VMEM((ROWS, D), BF),
                pltpu.VMEM(modulation.shape, F32),
                pltpu.VMEM((D, 3 * W), BF),
                pltpu.VMEM((ROWS, D), BF),
                pltpu.VMEM((ROWS, W), BF),
                pltpu.VMEM((ROWS, W), BF),
                pltpu.VMEM((W, ROWS), BF),
                pltpu.VMEM((TOK, W), BF),
                pltpu.VMEM((TOK, W), BF),
                pltpu.VMEM((W, TOK), BF),
                pltpu.VMEM((2, NX * W, W), BF),
                pltpu.VMEM((2, W // 2, W), BF),
                pltpu.VMEM((NC, C, NX * W), BF),
                pltpu.VMEM((NC, C, W), F32),
                pltpu.VMEM((NC, C, W), BF),
                pltpu.VMEM((NC, C, W), BF),
                pltpu.VMEM((2, TOK, W), BF),
                pltpu.VMEM((TOK + 16, W), F32),
                pltpu.VMEM((TOK, W), BF),
                pltpu.VMEM((nq, 16, W), BF),
                pltpu.VMEM((16, W), BF),
                dma((8,)), dma((2,)), dma((2,)), dma((9,)), dma((9,)),
                dma((NC, 4)), dma((NC, 4)), dma((NC,)), dma((NC,)),
                dma((2,)), dma((2,)), dma((nq,)), dma((1,)), dma,
            ],
            compiler_params=pltpu.CompilerParams(
                collective_id=0, has_side_effects=True, vmem_limit_bytes=56 * 1024 * 1024
            ),
        )(
            levels, frame_counts, sampler_coef, latents, modulation,
            jnp.transpose(w_qkv, (1, 0, 2)), w_out, fresh_noise,
        )

    return jax.shard_map(
        step,
        mesh=mesh,
        in_specs=(
            P("queue", None), P(None, "tp"), P("queue"), P("queue"), P(),
            P(None, None, "tp"), P("tp", None), P(),
        ),
        out_specs=(P("queue", "tp"), P("queue", "tp")),
        check_vma=False,
    )
```

time: 444 us -> 51 us (0.11)
  the two profiles are of different devices: /device:TPU:1 before, /device:TPU:2 now
where the time goes in v1:
time: 51 us; the launch traced here: 50.8 us
  Pallas kernels  45.9 us (90%)
  local copies, waits for them, and re-layouts  2.99 us (6%)
  between operations  1.93 us (4%)
    pallas_call x1, Pallas kernels, step(): pl.pallas_call(lambda *refs: kernel(nq, *refs), out_shape=(jax.ShapeDtype...  45.9 us
    unnamed x2, local copies, waits for them, and re-layouts  2.99 us

profile of v1, /device:TPU:2, one launch (start us, length us, event | category | flops | bytes accessed | tf_op | source)
XLA Modules:
  0.0 50.8 jit_solution(2172568675806264106)
XLA Ops:
  1.9 45.9 %shard_map.95 = (bf16[384,384]{1,0:T(8,128)(2,1)}, bf16[6,384]{1,0:T(8,128)(2,1)}) custom-call(s32[1]{0:T(128)S(6)} %copy.12.refs_0_, s32[1]{0:T(128)S(6)} %copy.13.refs_1_, f32[2,50]{1,0:T(2,128)} %refs_2_.1, bf16[384,3072]{1,0:T(8,128)(2,1)} %refs_3_.1, f32[50,2,3072]{2,1,0:T(2,128)} %refs_4_.1, bf16[3,3072,384]{2,1,0:T(8,128)(2,1)} %bitcast.1, ...), custom_call_target="tpu_custom_call" | custom-call | tf_op jit(solution)/shard_map/pallas_call | solution.py:384
  47.8 1.7 %copy.14 = bf16[384,384]{1,0:T(8,128)(2,1)} copy(bf16[384,384]{1,0:T(8,128)(2,1)} %get-tuple-element.4) | data formatting | bytes 589824
  49.5 1.3 %copy.15 = bf16[6,384]{1,0:T(8,128)(2,1)} copy(bf16[6,384]{1,0:T(8,128)(2,1)} %get-tuple-element.5) | data formatting | bytes 9216

commit v2 on v1

--- a/solution.py
+++ b/solution.py
@@ -21,16 +21,16 @@
 def kernel(
     nq, levels, counts, coef, lat_hbm, mod_hbm, wqkv_hbm, wout_hbm, fresh_hbm,
     out_ref, fin_ref,
-    lat, mod, wbuf, normed, qbuf, kown, vt, kpri, vpri, vtp, wo, fw, ag,
+    lat, mod, wbuf, normed, qbuf, kown, vt, kpri, vpri, vtp, wo, ag,
     acc, rsend, rrecv, f0, f0f, arr, finsrc, findst,
-    ld_sem, kv_s, kv_r, wo_s, wo_r, ag_s, ag_r, rs_s, rs_r, f_s, f_r, fin_s, fin_r, fresh_sem,
+    ld_sem, kv_s, kv_r, wo_s, wo_r, ag_s, ag_r, rs_s, rs_r, f_s, f_r, fin_s, fin_r, fresh_sem, here,
 ):
     q = lax.axis_index("queue")
     t = lax.axis_index("tp")
     x = lax.rem(t, NX)
     y = t // NX
     xr, xl, xo = lax.rem(x + 1, NX), lax.rem(x + 3, NX), lax.rem(x + 2, NX)
-    right, left = y * NX + xr, y * NX + xl
+    right, left, opposite = y * NX + xr, y * NX + xl, y * NX + xo
     ypeer = (1 - y) * NX + x
     core = lax.rem(q, 2)
     sib = q + 1 - 2 * core
@@ -53,53 +53,64 @@
     def col(block):
         return pl.ds(pl.multiple_of(block * W, 128), W)
 
-    ld_o = [load(wout_hbm.at[:, col(j * NX + x)], wo.at[j, pl.ds(0, W)], 6 + j) for j in range(2)]
+    def wblock(half, k):
+        return wout_hbm.at[:, col(half * NX + k)]
+
+    ld_o = [load(wblock(y, k), wo.at[k, pl.ds(0, W)], 6 + k) for k in range(NX)]
     for c in (ld_f1, ld_mod, ld_k, ld_v, ld_f0, ld_q, *ld_o):
         c.start()
 
     barrier = pltpu.get_barrier_semaphore()
-    for dev in ({"tp": right}, {"tp": left}, {"tp": ypeer}):
+
+    def hello(**dev):
         pl.semaphore_signal(barrier, inc=1, device_id=dev, device_id_type=MESH)
 
+    for peer in (right, left, opposite, ypeer):
+        hello(tp=peer)
+
+    @pl.when(q == 0)
+    def _():
+        def greet(i, _):
+            hello(queue=i)
+            return 0
+
+        lax.fori_loop(1, nq, greet, 0)
+
     @pl.when(q > 0)
     def _():
-        pl.semaphore_signal(barrier, inc=1, device_id={"queue": q - 1}, device_id_type=MESH)
-
-    @pl.when(q < nq - 1)
-    def _():
-        pl.semaphore_signal(barrier, inc=1, device_id={"queue": q + 1}, device_id_type=MESH)
-
-    @pl.when(q > 1)
-    def _():
-        pl.semaphore_signal(barrier, inc=1, device_id={"queue": 0}, device_id_type=MESH)
-
-    @pl.when(q == 0)
-    def _():
-        pl.semaphore_wait(barrier, 4 + nq - 2)
-
-    @pl.when((q > 0) & (q < nq - 1))
-    def _():
-        pl.semaphore_wait(barrier, 5)
-
-    @pl.when(q == nq - 1)
-    def _():
-        pl.semaphore_wait(barrier, 4)
-
-    wc = wo.at[core]
-    H = W // 2
-    opp = col(core * NX + xo)
-    wo_via_r = remote(wout_hbm.at[pl.ds(0, H), opp], fw.at[0], wo_s.at[2], wo_r.at[2], tp=right)
-    wo_via_l = remote(wout_hbm.at[pl.ds(H, H), opp], fw.at[1], wo_s.at[3], wo_r.at[3], tp=left)
-    wo_r1 = remote(wout_hbm.at[:, col(core * NX + xr)], wc.at[pl.ds(W, W)], wo_s.at[0], wo_r.at[0], tp=right)
-    wo_l1 = remote(wout_hbm.at[:, col(core * NX + xl)], wc.at[pl.ds(3 * W, W)], wo_s.at[1], wo_r.at[1], tp=left)
-    wo_fr = remote(fw.at[0], wc.at[pl.ds(2 * W, H)], wo_s.at[4], wo_r.at[4], tp=right)
-    wo_fl = remote(fw.at[1], wc.at[pl.ds(2 * W + H, H)], wo_s.at[5], wo_r.at[5], tp=left)
-    wo_sib = [
-        remote(wc.at[pl.ds(s * W, W)], wc.at[pl.ds(s * W, W)], wo_s.at[5 + s], wo_r.at[5 + s], queue=sib)
-        for s in (1, 2, 3)
-    ]
-    for c in (wo_via_r, wo_via_l, wo_r1, wo_l1):
-        c.start()
+        hello(queue=q - 1)
+
+        @pl.when(q < nq - 1)
+        def _():
+            hello(queue=q + 1)
+
+    def meet():
+        @pl.when(q == 0)
+        def _():
+            pl.semaphore_wait(barrier, 5)
+
+        @pl.when(q == 1)
+        def _():
+            pl.semaphore_wait(barrier, 6)
+
+        @pl.when((q > 1) & (q < nq - 1))
+        def _():
+            pl.semaphore_wait(barrier, 7)
+
+        @pl.when(q == nq - 1)
+        def _():
+            pl.semaphore_wait(barrier, 6)
+
+        @pl.when(q > 0)
+        def _():
+            pl.semaphore_signal(here, inc=1, device_id={"queue": 0}, device_id_type=MESH)
+
+    wo_y, wo_sib = [], []
+    for i in range(2):
+        k = 2 * core + i
+        low = wo.at[k, pl.ds(W, W)]
+        wo_y.append(remote(wblock(1 - y, k), low, wo_s.at[i], wo_r.at[i], tp=ypeer))
+        wo_sib.append(remote(low, low, wo_s.at[2 + i], wo_r.at[2 + i], queue=sib))
 
     level = levels[0]
     count = counts[0]
@@ -138,11 +149,14 @@
     kown[pl.ds(TOK, TOK), pl.ds(0, 256)] = mm(TOK, TOK, 0, 256)
     mid = mm(TOK, TOK, 256, 256)
     kown[pl.ds(TOK, TOK), pl.ds(256, 128)] = mid[:, :128]
+    meet()
 
     @pl.when(q < nq - 1)
     def _():
         kv_k.start()
 
+    for c in wo_y:
+        c.start()
     f0[1, :, pl.ds(0, 128)] = mid[:, 128:]
     f0[1, :, pl.ds(128, 256)] = mm(TOK, TOK, 512, 256)
 
@@ -157,11 +171,6 @@
 
     ld_f0.wait()
     norm(0)
-
-    wo_via_r.wait_recv()
-    wo_fr.start()
-    wo_via_l.wait_recv()
-    wo_fl.start()
 
     ld_q.wait()
     qbuf[:, pl.ds(0, 256)] = mm(0, ROWS, 2 * W, 256) * BF(0.125)
@@ -206,43 +215,31 @@
         ot = jnp.where(row < 64, o[:, :C], o[:, C:])
         ag[r, :, lanes] = ot.T.astype(BF)
 
-    ag_dir, ag_fwd = [], []
-    for r in range(NC):
-        own = ag.at[r, :, pl.ds(0, W)]
-        ag_dir.append((
-            remote(own, ag.at[r, :, pl.ds(W, W)], ag_s.at[r, 0], ag_r.at[r, 0], tp=right),
-            remote(own, ag.at[r, :, pl.ds(3 * W, W)], ag_s.at[r, 1], ag_r.at[r, 1], tp=left),
-        ))
-        top_half, low_half = pl.ds(0, C // 2), pl.ds(C // 2, C // 2)
-        ag_fwd.append((
-            remote(ag.at[r, top_half, pl.ds(W, W)], ag.at[r, top_half, pl.ds(2 * W, W)],
-                   ag_s.at[r, 2], ag_r.at[r, 2], tp=right),
-            remote(ag.at[r, low_half, pl.ds(3 * W, W)], ag.at[r, low_half, pl.ds(2 * W, W)],
-                   ag_s.at[r, 3], ag_r.at[r, 3], tp=left),
-        ))
-
-    def ag_start(r):
-        for c in ag_dir[r]:
+    ag_y = [
+        remote(ag.at[r, :, pl.ds(0, W)], ag.at[r, :, pl.ds(W, W)], ag_s.at[r], ag_r.at[r], tp=ypeer)
+        for r in range(NC)
+    ]
+    rs = [
+        [
+            (k, remote(rsend.at[r, i], rrecv.at[r, i], rs_s.at[r, i], rs_r.at[r, i], tp=dev))
+            for i, (k, dev) in enumerate(((xo, opposite), (xr, right), (xl, left)))
+        ]
+        for r in range(NC)
+    ]
+
+    def proj(r):
+        ag_y[r].wait_recv()
+        a = ag[r]
+        for i, (k, c) in enumerate(rs[r]):
+            rsend[r, i] = jnp.dot(a, wo[k], preferred_element_type=F32).astype(BF)
             c.start()
-
-    def ag_forward(r):
-        for got, on in zip(ag_dir[r], ag_fwd[r]):
-            got.wait_recv()
-            on.start()
-
-    rs = [remote(rsend.at[r], rrecv.at[r], rs_s.at[r], rs_r.at[r], tp=ypeer) for r in range(NC)]
-
-    def proj(r):
-        for c in ag_fwd[r]:
+        acc[r] = jnp.dot(a, wo[x], preferred_element_type=F32)
+
+    def final(r):
+        branch = acc[r]
+        for i, (_, c) in enumerate(rs[r]):
             c.wait_recv()
-        a = ag[r]
-        rsend[r] = jnp.dot(a, wo[1 - y], preferred_element_type=F32).astype(BF)
-        rs[r].start()
-        acc[r] = jnp.dot(a, wo[y], preferred_element_type=F32)
-
-    def final(r):
-        rs[r].wait_recv()
-        branch = acc[r] + rrecv[r].astype(F32)
+            branch = branch + rrecv[r, i].astype(F32)
         cur = lat[pl.ds(r * C, C), col(t)].astype(F32)
         upd = c_lat * cur + c_out * (cur + branch)
         if r == 0:
@@ -264,31 +261,23 @@
 
     for p in range(3):
         att_pair(0, p)
-    ag_start(0)
-    wo_r1.wait_recv()
-    wo_sib[0].start()
+    ag_y[0].start()
+    for got, on in zip(wo_y, wo_sib):
+        got.wait_recv()
+        on.start()
     for p in range(3):
         att_pair(1, p)
-        if p == 0:
-            ag_forward(0)
-    ag_start(1)
-    wo_l1.wait_recv()
-    wo_sib[2].start()
-    wo_fr.wait_recv()
-    wo_fl.wait_recv()
-    wo_sib[1].start()
-    att_pair(2, 0)
-    ag_forward(1)
+    ag_y[1].start()
     for c in ld_o:
         c.wait()
     for c in wo_sib:
         c.wait_recv()
     proj(0)
-    att_pair(2, 1)
-    att_pair(2, 2)
-    ag_start(2)
+    for p in range(3):
+        att_pair(2, p)
+    ag_y[2].start()
     proj(1)
-    ag_forward(2)
+    proj(2)
 
     f_a = remote(f0.at[0, pl.ds(0, C)], arr.at[pl.ds(0, C)], f_s.at[0], f_r.at[0], queue=q - 1)
     f_b = remote(
@@ -308,7 +297,6 @@
     def _():
         f_a.start()
 
-    proj(2)
     u = final(1)
     f0[0, pl.ds(C, TOK - C)] = u[: TOK - C].astype(BF)
     f0f[pl.ds(C, TOK - C)] = u[: TOK - C]
@@ -333,6 +321,7 @@
             fin_copy(i).start()
             return 0
 
+        pl.semaphore_wait(here, nq - 1)
         lax.fori_loop(1, nq, go, 0)
 
     out_ref[pl.ds(2 * C - TOK, C)] = final(2).astype(BF)
@@ -366,10 +355,10 @@
         fresh.wait()
 
     out_ref[pl.ds(TOK, TOK)] = arr[...]
-    for c in (wo_via_r, wo_via_l, wo_r1, wo_l1, wo_fr, wo_fl, *wo_sib, *rs):
+    for c in (*wo_y, *wo_sib, *ag_y):
         c.wait_send()
     for r in range(NC):
-        for c in (*ag_dir[r], *ag_fwd[r]):
+        for _, c in rs[r]:
             c.wait_send()
 
 
@@ -400,20 +389,19 @@
                 pltpu.VMEM((TOK, W), BF),
                 pltpu.VMEM((TOK, W), BF),
                 pltpu.VMEM((W, TOK), BF),
-                pltpu.VMEM((2, NX * W, W), BF),
-                pltpu.VMEM((2, W // 2, W), BF),
-                pltpu.VMEM((NC, C, NX * W), BF),
+                pltpu.VMEM((NX, 2 * W, W), BF),
+                pltpu.VMEM((NC, C, 2 * W), BF),
                 pltpu.VMEM((NC, C, W), F32),
-                pltpu.VMEM((NC, C, W), BF),
-                pltpu.VMEM((NC, C, W), BF),
+                pltpu.VMEM((NC, 3, C, W), BF),
+                pltpu.VMEM((NC, 3, C, W), BF),
                 pltpu.VMEM((2, TOK, W), BF),
                 pltpu.VMEM((TOK + 16, W), F32),
                 pltpu.VMEM((TOK, W), BF),
                 pltpu.VMEM((nq, 16, W), BF),
                 pltpu.VMEM((16, W), BF),
-                dma((8,)), dma((2,)), dma((2,)), dma((9,)), dma((9,)),
-                dma((NC, 4)), dma((NC, 4)), dma((NC,)), dma((NC,)),
-                dma((2,)), dma((2,)), dma((nq,)), dma((1,)), dma,
+                dma((10,)), dma((2,)), dma((2,)), dma((4,)), dma((4,)),
+                dma((NC,)), dma((NC,)), dma((NC, 3)), dma((NC, 3)),
+                dma((2,)), dma((2,)), dma((nq,)), dma((1,)), dma, pltpu.SemaphoreType.REGULAR,
             ],
             compiler_params=pltpu.CompilerParams(
                 collective_id=0, has_side_effects=True, vmem_limit_bytes=56 * 1024 * 1024

time: 51 us -> 54.2 us (1.063)
  the two profiles are of different devices: /device:TPU:2 before, /device:TPU:1 now
where the time goes in v2:
time: 54.2 us; the launch traced here: 54 us
  Pallas kernels  49.1 us (91%)
  local copies, waits for them, and re-layouts  2.99 us (6%)
  between operations  1.93 us (4%)
    pallas_call x1, Pallas kernels, step(): pl.pallas_call(lambda *refs: kernel(nq, *refs), out_shape=(jax.ShapeDtype...  49.1 us
    unnamed x2, local copies, waits for them, and re-layouts  2.99 us

profile of v2, /device:TPU:1, one launch (start us, length us, event | category | flops | bytes accessed | tf_op | source)
XLA Modules:
  0.0 54.0 jit_solution(2374503540581846264)
XLA Ops:
  1.9 49.1 %shard_map.95 = (bf16[384,384]{1,0:T(8,128)(2,1)}, bf16[6,384]{1,0:T(8,128)(2,1)}) custom-call(s32[1]{0:T(128)S(6)} %copy.12.refs_0_, s32[1]{0:T(128)S(6)} %copy.13.refs_1_, f32[2,50]{1,0:T(2,128)} %refs_2_.1, bf16[384,3072]{1,0:T(8,128)(2,1)} %refs_3_.1, f32[50,2,3072]{2,1,0:T(2,128)} %refs_4_.1, bf16[3,3072,384]{2,1,0:T(8,128)(2,1)} %bitcast.1, ...), custom_call_target="tpu_custom_call" | custom-call | tf_op jit(solution)/shard_map/pallas_call | solution.py:373
  51.0 1.7 %copy.14 = bf16[384,384]{1,0:T(8,128)(2,1)} copy(bf16[384,384]{1,0:T(8,128)(2,1)} %get-tuple-element.4) | data formatting | bytes 589824
  52.7 1.3 %copy.15 = bf16[6,384]{1,0:T(8,128)(2,1)} copy(bf16[6,384]{1,0:T(8,128)(2,1)} %get-tuple-element.5) | data formatting | bytes 9216

commit v3 on v2

--- a/solution.py
+++ b/solution.py
@@ -21,7 +21,7 @@
 def kernel(
     nq, levels, counts, coef, lat_hbm, mod_hbm, wqkv_hbm, wout_hbm, fresh_hbm,
     out_ref, fin_ref,
-    lat, mod, wbuf, normed, qbuf, kown, vt, kpri, vpri, vtp, wo, ag,
+    lat, mod, wbuf, normed, qbuf, kown, vt, kpri, vpri, vtp, wo, wst, ag,
     acc, rsend, rrecv, f0, f0f, arr, finsrc, findst,
     ld_sem, kv_s, kv_r, wo_s, wo_r, ag_s, ag_r, rs_s, rs_r, f_s, f_r, fin_s, fin_r, fresh_sem, here,
 ):
@@ -34,6 +34,7 @@
     ypeer = (1 - y) * NX + x
     core = lax.rem(q, 2)
     sib = q + 1 - 2 * core
+    q_other = q + 2 - 4 * (lax.rem(q, 4) // 2)
 
     def load(src, dst, i):
         return pltpu.make_async_copy(src, dst, ld_sem.at[i])
@@ -44,7 +45,9 @@
         )
 
     ld_f1 = load(lat_hbm.at[pl.ds(TOK, TOK)], lat.at[pl.ds(TOK, TOK)], 0)
-    ld_mod = load(mod_hbm, mod, 1)
+    n_levels = mod_hbm.shape[0]
+    first = jnp.clip(q * (n_levels - 1) // (nq - 1) - 1, 0, n_levels - 3)
+    ld_mod = load(mod_hbm.at[pl.ds(first, 3)], mod, 1)
     ld_k = load(wqkv_hbm.at[1], wbuf.at[:, pl.ds(0, W)], 2)
     ld_v = load(wqkv_hbm.at[2], wbuf.at[:, pl.ds(W, W)], 3)
     ld_f0 = load(lat_hbm.at[pl.ds(0, TOK)], lat.at[pl.ds(0, TOK)], 4)
@@ -57,7 +60,8 @@
         return wout_hbm.at[:, col(half * NX + k)]
 
     ld_o = [load(wblock(y, k), wo.at[k, pl.ds(0, W)], 6 + k) for k in range(NX)]
-    for c in (ld_f1, ld_mod, ld_k, ld_v, ld_f0, ld_q, *ld_o):
+    ld_w = [load(wblock(1 - y, 2 * core + i), wst.at[i], 10 + i) for i in range(2)]
+    for c in (ld_f1, ld_mod, *ld_w, ld_k, ld_v, ld_f0, ld_q, *ld_o):
         c.start()
 
     barrier = pltpu.get_barrier_semaphore()
@@ -67,6 +71,7 @@
 
     for peer in (right, left, opposite, ypeer):
         hello(tp=peer)
+    hello(tp=ypeer, queue=q_other)
 
     @pl.when(q == 0)
     def _():
@@ -87,19 +92,19 @@
     def meet():
         @pl.when(q == 0)
         def _():
-            pl.semaphore_wait(barrier, 5)
+            pl.semaphore_wait(barrier, 6)
 
         @pl.when(q == 1)
         def _():
-            pl.semaphore_wait(barrier, 6)
+            pl.semaphore_wait(barrier, 7)
 
         @pl.when((q > 1) & (q < nq - 1))
         def _():
+            pl.semaphore_wait(barrier, 8)
+
+        @pl.when(q == nq - 1)
+        def _():
             pl.semaphore_wait(barrier, 7)
-
-        @pl.when(q == nq - 1)
-        def _():
-            pl.semaphore_wait(barrier, 6)
 
         @pl.when(q > 0)
         def _():
@@ -109,7 +114,7 @@
     for i in range(2):
         k = 2 * core + i
         low = wo.at[k, pl.ds(W, W)]
-        wo_y.append(remote(wblock(1 - y, k), low, wo_s.at[i], wo_r.at[i], tp=ypeer))
+        wo_y.append(remote(wst.at[i], low, wo_s.at[i], wo_r.at[i], tp=ypeer, queue=(q, q_other)[i]))
         wo_sib.append(remote(low, low, wo_s.at[2 + i], wo_r.at[2 + i], queue=sib))
 
     level = levels[0]
@@ -119,7 +124,7 @@
     c_out = coef[1, level]
 
     def norm(start):
-        table = mod[level]
+        table = mod[jnp.clip(level - first, 0, 2)]
         gain = 1.0 + table[1:2]
         shift = table[0:1]
 
@@ -143,20 +148,21 @@
 
     ld_f1.wait()
     ld_mod.wait()
+    meet()
+    for c, l in zip(wo_y, ld_w):
+        l.wait()
+        c.start()
     norm(TOK)
     ld_k.wait()
     ld_v.wait()
     kown[pl.ds(TOK, TOK), pl.ds(0, 256)] = mm(TOK, TOK, 0, 256)
     mid = mm(TOK, TOK, 256, 256)
     kown[pl.ds(TOK, TOK), pl.ds(256, 128)] = mid[:, :128]
-    meet()
 
     @pl.when(q < nq - 1)
     def _():
         kv_k.start()
 
-    for c in wo_y:
-        c.start()
     f0[1, :, pl.ds(0, 128)] = mid[:, 128:]
     f0[1, :, pl.ds(128, 256)] = mm(TOK, TOK, 512, 256)
 
@@ -187,7 +193,7 @@
     even = (lane < 64).astype(F32)
     odd = 1.0 - even
 
-    def att_pair(r, p):
+    def weigh(r, p):
         lanes = pl.ds(p * 128, 128)
         qp = qbuf[pl.ds(r * C, C), lanes].astype(F32)
         qs = jnp.concatenate([qp * even, qp * odd], axis=0).astype(BF)
@@ -209,11 +215,17 @@
         )
         inv = 1.0 / total
         w_own = jnp.concatenate([(e0 * inv).astype(BF), (e1 * inv).astype(BF)], axis=0)
-        w_pri = (ep * inv).astype(BF)
+        return w_own, (ep * inv).astype(BF)
+
+    def attend(r, p, w_own, w_pri):
+        lanes = pl.ds(p * 128, 128)
         o = jnp.dot(vt[lanes, :], w_own, preferred_element_type=F32)
         o = o + jnp.dot(vtp[lanes, :], w_pri, preferred_element_type=F32)
         ot = jnp.where(row < 64, o[:, :C], o[:, C:])
         ag[r, :, lanes] = ot.T.astype(BF)
+
+    def att_pair(r, p):
+        attend(r, p, *weigh(r, p))
 
     ag_y = [
         remote(ag.at[r, :, pl.ds(0, W)], ag.at[r, :, pl.ds(W, W)], ag_s.at[r], ag_r.at[r], tp=ypeer)
@@ -255,12 +267,17 @@
     @pl.when(q > 0)
     def _():
         kv_k.wait_recv()
+
+    got = weigh(0, 0)
+
+    @pl.when(q > 0)
+    def _():
         kv_v.wait_recv()
 
     vtp[...] = vpri[...].T
-
-    for p in range(3):
-        att_pair(0, p)
+    attend(0, 0, *got)
+    att_pair(0, 1)
+    att_pair(0, 2)
     ag_y[0].start()
     for got, on in zip(wo_y, wo_sib):
         got.wait_recv()
@@ -270,11 +287,12 @@
     ag_y[1].start()
     for c in ld_o:
         c.wait()
+    att_pair(2, 0)
     for c in wo_sib:
         c.wait_recv()
     proj(0)
-    for p in range(3):
-        att_pair(2, p)
+    att_pair(2, 1)
+    att_pair(2, 2)
     ag_y[2].start()
     proj(1)
     proj(2)
@@ -372,15 +390,12 @@
         dma = pltpu.SemaphoreType.DMA
         return pl.pallas_call(
             lambda *refs: kernel(nq, *refs),
-            out_shape=(
-                jax.ShapeDtypeStruct((ROWS, W), BF),
-                jax.ShapeDtypeStruct((TOK // nq, W), BF),
-            ),
+            out_shape=(pltpu.VMEM((ROWS, W), BF), pltpu.VMEM((TOK // nq, W), BF)),
             in_specs=[smem, smem, smem] + [anyspace] * 5,
             out_specs=(vmem, vmem),
             scratch_shapes=[
                 pltpu.VMEM((ROWS, D), BF),
-                pltpu.VMEM(modulation.shape, F32),
+                pltpu.VMEM((3,) + modulation.shape[1:], F32),
                 pltpu.VMEM((D, 3 * W), BF),
                 pltpu.VMEM((ROWS, D), BF),
                 pltpu.VMEM((ROWS, W), BF),
@@ -390,6 +405,7 @@
                 pltpu.VMEM((TOK, W), BF),
                 pltpu.VMEM((W, TOK), BF),
                 pltpu.VMEM((NX, 2 * W, W), BF),
+                pltpu.VMEM((2, W, W), BF),
                 pltpu.VMEM((NC, C, 2 * W), BF),
                 pltpu.VMEM((NC, C, W), F32),
                 pltpu.VMEM((NC, 3, C, W), BF),
@@ -399,7 +415,7 @@
                 pltpu.VMEM((TOK, W), BF),
                 pltpu.VMEM((nq, 16, W), BF),
                 pltpu.VMEM((16, W), BF),
-                dma((10,)), dma((2,)), dma((2,)), dma((4,)), dma((4,)),
+                dma((12,)), dma((2,)), dma((2,)), dma((4,)), dma((4,)),
                 dma((NC,)), dma((NC,)), dma((NC, 3)), dma((NC, 3)),
                 dma((2,)), dma((2,)), dma((nq,)), dma((1,)), dma, pltpu.SemaphoreType.REGULAR,
             ],

time: 54.2 us -> 43.1 us (0.80)
  Pallas kernels: 49.1 us -> 39.8 us
  local copies, waits for them, and re-layouts: 2.99 us -> 1.31 us
    pallas_call x1, Pallas kernels: 49.1 us -> 39.8 us  [step(): pl.pallas_call(lambda *refs: kernel(nq, *refs), out_shape=(pltpu.VMEM((RO...]
    unnamed x2, local copies, waits for them, and re-layouts: 2.99 us -> 1.31 us
where the time goes in v3:
time: 43.1 us; the launch traced here: 43 us
  Pallas kernels  39.8 us (92%)
  between operations  1.93 us (4%)
  local copies, waits for them, and re-layouts  1.31 us (3%)
    pallas_call x1, Pallas kernels, step(): pl.pallas_call(lambda *refs: kernel(nq, *refs), out_shape=(pltpu.VMEM((RO...  39.8 us
    unnamed x2, local copies, waits for them, and re-layouts  1.31 us

profile of v3, /device:TPU:1, one launch (start us, length us, event | category | flops | bytes accessed | tf_op | source)
XLA Modules:
  0.0 43.0 jit_solution(1444699575639596567)
XLA Ops:
  1.9 39.8 %shard_map.95 = (bf16[384,384]{1,0:T(8,128)(2,1)S(1)}, bf16[6,384]{1,0:T(8,128)(2,1)S(1)}) custom-call(s32[1]{0:T(128)S(6)} %copy.14.refs_0_, s32[1]{0:T(128)S(6)} %copy.15.refs_1_, f32[2,50]{1,0:T(2,128)} %refs_2_.1, bf16[384,3072]{1,0:T(8,128)(2,1)} %refs_3_.1, f32[50,2,3072]{2,1,0:T(2,128)} %refs_4_.1, bf16[3,3072,384]{2,1,0:T(8,128)(2,1)} %bitcast.1, ...), custom_call_target="tpu_custom_call" | custom-call | tf_op jit(solution)/shard_map/pallas_call | solution.py:391
  41.7 0.7 %copy.12 = bf16[384,384]{1,0:T(8,128)(2,1)} copy(bf16[384,384]{1,0:T(8,128)(2,1)S(1)} %get-tuple-element.2) | data formatting | bytes 589824
  42.4 0.6 %copy.13 = bf16[6,384]{1,0:T(8,128)(2,1)} copy(bf16[6,384]{1,0:T(8,128)(2,1)S(1)} %get-tuple-element.3) | data formatting | bytes 9216

commit v4 on v3

--- a/solution.py
+++ b/solution.py
@@ -22,8 +22,8 @@
     nq, levels, counts, coef, lat_hbm, mod_hbm, wqkv_hbm, wout_hbm, fresh_hbm,
     out_ref, fin_ref,
     lat, mod, wbuf, normed, qbuf, kown, vt, kpri, vpri, vtp, wo, wst, ag,
-    acc, rsend, rrecv, f0, f0f, arr, finsrc, findst,
-    ld_sem, kv_s, kv_r, wo_s, wo_r, ag_s, ag_r, rs_s, rs_r, f_s, f_r, fin_s, fin_r, fresh_sem, here,
+    acc, osend, orecv, rsend, rrecv, f0, f0f, arr, finsrc, findst,
+    ld_sem, kv_s, kv_r, wo_s, wo_r, ag_s, ag_r, o_s, o_r, rs_s, rs_r, f_s, f_r, fin_s, fin_r, fresh_sem, here,
 ):
     q = lax.axis_index("queue")
     t = lax.axis_index("tp")
@@ -231,25 +231,46 @@
         remote(ag.at[r, :, pl.ds(0, W)], ag.at[r, :, pl.ds(W, W)], ag_s.at[r], ag_r.at[r], tp=ypeer)
         for r in range(NC)
     ]
+    half = C // 2
+    top_half, low_half = pl.ds(0, half), pl.ds(half, half)
+    opp = [
+        (
+            remote(osend.at[r, top_half], orecv.at[r, top_half], o_s.at[r, 0], o_r.at[r, 0], tp=right),
+            remote(osend.at[r, low_half], orecv.at[r, low_half], o_s.at[r, 1], o_r.at[r, 1], tp=left),
+        )
+        for r in range(NC)
+    ]
     rs = [
         [
-            (k, remote(rsend.at[r, i], rrecv.at[r, i], rs_s.at[r, i], rs_r.at[r, i], tp=dev))
-            for i, (k, dev) in enumerate(((xo, opposite), (xr, right), (xl, left)))
+            remote(rsend.at[r, i], rrecv.at[r, i], rs_s.at[r, i], rs_r.at[r, i], tp=dev)
+            for i, dev in enumerate((right, left))
         ]
         for r in range(NC)
     ]
 
+    def proj_opp(r):
+        ag_y[r].wait_recv()
+        osend[r] = jnp.dot(ag[r], wo[xo], preferred_element_type=F32).astype(BF)
+        for c in opp[r]:
+            c.start()
+
     def proj(r):
-        ag_y[r].wait_recv()
         a = ag[r]
-        for i, (k, c) in enumerate(rs[r]):
-            rsend[r, i] = jnp.dot(a, wo[k], preferred_element_type=F32).astype(BF)
-            c.start()
+        to_right = jnp.dot(a, wo[xr], preferred_element_type=F32)
+        to_left = jnp.dot(a, wo[xl], preferred_element_type=F32)
+        opp[r][0].wait_recv()
+        rsend[r, 0, top_half] = (to_right[:half] + orecv[r, top_half].astype(F32)).astype(BF)
+        rsend[r, 0, low_half] = to_right[half:].astype(BF)
+        rs[r][0].start()
+        opp[r][1].wait_recv()
+        rsend[r, 1, top_half] = to_left[:half].astype(BF)
+        rsend[r, 1, low_half] = (to_left[half:] + orecv[r, low_half].astype(F32)).astype(BF)
+        rs[r][1].start()
         acc[r] = jnp.dot(a, wo[x], preferred_element_type=F32)
 
     def final(r):
         branch = acc[r]
-        for i, (_, c) in enumerate(rs[r]):
+        for i, c in enumerate(rs[r]):
             c.wait_recv()
             branch = branch + rrecv[r, i].astype(F32)
         cur = lat[pl.ds(r * C, C), col(t)].astype(F32)
@@ -275,25 +296,36 @@
         kv_v.wait_recv()
 
     vtp[...] = vpri[...].T
+    nxt = weigh(0, 1)
     attend(0, 0, *got)
-    att_pair(0, 1)
-    att_pair(0, 2)
+    last = weigh(0, 2)
+    attend(0, 1, *nxt)
+    attend(0, 2, *last)
     ag_y[0].start()
     for got, on in zip(wo_y, wo_sib):
         got.wait_recv()
         on.start()
-    for p in range(3):
-        att_pair(1, p)
+    got = weigh(1, 0)
+    nxt = weigh(1, 1)
+    attend(1, 0, *got)
+    last = weigh(1, 2)
+    attend(1, 1, *nxt)
+    attend(1, 2, *last)
     ag_y[1].start()
     for c in ld_o:
         c.wait()
     att_pair(2, 0)
     for c in wo_sib:
         c.wait_recv()
+    proj_opp(0)
+    nxt = weigh(2, 1)
+    last = weigh(2, 2)
+    attend(2, 1, *nxt)
+    attend(2, 2, *last)
+    ag_y[2].start()
+    proj_opp(1)
     proj(0)
-    att_pair(2, 1)
-    att_pair(2, 2)
-    ag_y[2].start()
+    proj_opp(2)
     proj(1)
     proj(2)
 
@@ -376,7 +408,7 @@
     for c in (*wo_y, *wo_sib, *ag_y):
         c.wait_send()
     for r in range(NC):
-        for _, c in rs[r]:
+        for c in (*opp[r], *rs[r]):
             c.wait_send()
 
 
@@ -408,15 +440,17 @@
                 pltpu.VMEM((2, W, W), BF),
                 pltpu.VMEM((NC, C, 2 * W), BF),
                 pltpu.VMEM((NC, C, W), F32),
-                pltpu.VMEM((NC, 3, C, W), BF),
-                pltpu.VMEM((NC, 3, C, W), BF),
+                pltpu.VMEM((NC, C, W), BF),
+                pltpu.VMEM((NC, C, W), BF),
+                pltpu.VMEM((NC, 2, C, W), BF),
+                pltpu.VMEM((NC, 2, C, W), BF),
                 pltpu.VMEM((2, TOK, W), BF),
                 pltpu.VMEM((TOK + 16, W), F32),
                 pltpu.VMEM((TOK, W), BF),
                 pltpu.VMEM((nq, 16, W), BF),
                 pltpu.VMEM((16, W), BF),
                 dma((12,)), dma((2,)), dma((2,)), dma((4,)), dma((4,)),
-                dma((NC,)), dma((NC,)), dma((NC, 3)), dma((NC, 3)),
+                dma((NC,)), dma((NC,)), dma((NC, 2)), dma((NC, 2)), dma((NC, 2)), dma((NC, 2)),
                 dma((2,)), dma((2,)), dma((nq,)), dma((1,)), dma, pltpu.SemaphoreType.REGULAR,
             ],
             compiler_params=pltpu.CompilerParams(

time: 43.1 us -> 42.5 us (0.986)
  Pallas kernels: 39.8 us -> 39.2 us
    pallas_call x1, Pallas kernels: 39.8 us -> 39.2 us  [step(): pl.pallas_call(lambda *refs: kernel(nq, *refs), out_shape=(pltpu.VMEM((RO...]
where the time goes in v4:
time: 42.5 us; the launch traced here: 42.4 us
  Pallas kernels  39.2 us (92%)
  between operations  1.93 us (5%)
  local copies, waits for them, and re-layouts  1.31 us (3%)
    pallas_call x1, Pallas kernels, step(): pl.pallas_call(lambda *refs: kernel(nq, *refs), out_shape=(pltpu.VMEM((RO...  39.2 us
    unnamed x2, local copies, waits for them, and re-layouts  1.31 us

profile of v4, /device:TPU:1, one launch (start us, length us, event | category | flops | bytes accessed | tf_op | source)
XLA Modules:
  0.0 42.4 jit_solution(7091316395072081377)
XLA Ops:
  1.9 39.2 %shard_map.95 = (bf16[384,384]{1,0:T(8,128)(2,1)S(1)}, bf16[6,384]{1,0:T(8,128)(2,1)S(1)}) custom-call(s32[1]{0:T(128)S(6)} %copy.14.refs_0_, s32[1]{0:T(128)S(6)} %copy.15.refs_1_, f32[2,50]{1,0:T(2,128)} %refs_2_.1, bf16[384,3072]{1,0:T(8,128)(2,1)} %refs_3_.1, f32[50,2,3072]{2,1,0:T(2,128)} %refs_4_.1, bf16[3,3072,384]{2,1,0:T(8,128)(2,1)} %bitcast.1, ...), custom_call_target="tpu_custom_call" | custom-call | tf_op jit(solution)/shard_map/pallas_call | solution.py:423
  41.1 0.7 %copy.12 = bf16[384,384]{1,0:T(8,128)(2,1)} copy(bf16[384,384]{1,0:T(8,128)(2,1)S(1)} %get-tuple-element.2) | data formatting | bytes 589824
  41.8 0.6 %copy.13 = bf16[6,384]{1,0:T(8,128)(2,1)} copy(bf16[6,384]{1,0:T(8,128)(2,1)S(1)} %get-tuple-element.3) | data formatting | bytes 9216

commit v5 on v4

--- a/solution.py
+++ b/solution.py
@@ -327,7 +327,6 @@
     proj(0)
     proj_opp(2)
     proj(1)
-    proj(2)
 
     f_a = remote(f0.at[0, pl.ds(0, C)], arr.at[pl.ds(0, C)], f_s.at[0], f_r.at[0], queue=q - 1)
     f_b = remote(
@@ -347,6 +346,7 @@
     def _():
         f_a.start()
 
+    proj(2)
     u = final(1)
     f0[0, pl.ds(C, TOK - C)] = u[: TOK - C].astype(BF)
     f0f[pl.ds(C, TOK - C)] = u[: TOK - C]

time: 42.5 us -> 42.2 us (level)
  no operation moved by 1% of the time
where the time goes in v5:
time: 42.2 us; the launch traced here: 42.1 us
  Pallas kernels  38.9 us (92%)
  between operations  1.93 us (5%)
  local copies, waits for them, and re-layouts  1.31 us (3%)
    pallas_call x1, Pallas kernels, step(): pl.pallas_call(lambda *refs: kernel(nq, *refs), out_shape=(pltpu.VMEM((RO...  38.9 us
    unnamed x2, local copies, waits for them, and re-layouts  1.31 us

profile of v5, /device:TPU:1, one launch (start us, length us, event | category | flops | bytes accessed | tf_op | source)
XLA Modules:
  0.0 42.1 jit_solution(12274227302029161474)
XLA Ops:
  1.9 38.9 %shard_map.95 = (bf16[384,384]{1,0:T(8,128)(2,1)S(1)}, bf16[6,384]{1,0:T(8,128)(2,1)S(1)}) custom-call(s32[1]{0:T(128)S(6)} %copy.14.refs_0_, s32[1]{0:T(128)S(6)} %copy.15.refs_1_, f32[2,50]{1,0:T(2,128)} %refs_2_.1, bf16[384,3072]{1,0:T(8,128)(2,1)} %refs_3_.1, f32[50,2,3072]{2,1,0:T(2,128)} %refs_4_.1, bf16[3,3072,384]{2,1,0:T(8,128)(2,1)} %bitcast.1, ...), custom_call_target="tpu_custom_call" | custom-call | tf_op jit(solution)/shard_map/pallas_call | solution.py:423
  40.8 0.7 %copy.12 = bf16[384,384]{1,0:T(8,128)(2,1)} copy(bf16[384,384]{1,0:T(8,128)(2,1)S(1)} %get-tuple-element.2) | data formatting | bytes 589824
  41.5 0.6 %copy.13 = bf16[6,384]{1,0:T(8,128)(2,1)} copy(bf16[6,384]{1,0:T(8,128)(2,1)S(1)} %get-tuple-element.3) | data formatting | bytes 9216

commit v6 on v5

--- a/solution.py
+++ b/solution.py
@@ -340,21 +340,23 @@
 
     u = final(0)
     f0[0, pl.ds(0, C)] = u.astype(BF)
+
+    @pl.when(q > 0)
+    def _():
+        f_a.start()
+
     f0f[pl.ds(0, C)] = u
-
-    @pl.when(q > 0)
-    def _():
-        f_a.start()
 
     proj(2)
     u = final(1)
     f0[0, pl.ds(C, TOK - C)] = u[: TOK - C].astype(BF)
+
+    @pl.when(q > 0)
+    def _():
+        f_b.start()
+
     f0f[pl.ds(C, TOK - C)] = u[: TOK - C]
     out_ref[pl.ds(0, 2 * C - TOK)] = u[TOK - C :].astype(BF)
-
-    @pl.when(q > 0)
-    def _():
-        f_b.start()
 
     share = TOK // nq
 

time: 42.2 us -> 42.2 us (level)
  no operation moved by 1% of the time
where the time goes in v6:
time: 42.2 us; the launch traced here: 42.1 us
  Pallas kernels  38.8 us (92%)
  between operations  1.93 us (5%)
  local copies, waits for them, and re-layouts  1.31 us (3%)
    pallas_call x1, Pallas kernels, step(): pl.pallas_call(lambda *refs: kernel(nq, *refs), out_shape=(pltpu.VMEM((RO...  38.8 us
    unnamed x2, local copies, waits for them, and re-layouts  1.31 us

profile of v6, /device:TPU:1, one launch (start us, length us, event | category | flops | bytes accessed | tf_op | source)
XLA Modules:
  0.0 42.1 jit_solution(18200791326351637831)
XLA Ops:
  1.9 38.8 %shard_map.95 = (bf16[384,384]{1,0:T(8,128)(2,1)S(1)}, bf16[6,384]{1,0:T(8,128)(2,1)S(1)}) custom-call(s32[1]{0:T(128)S(6)} %copy.14.refs_0_, s32[1]{0:T(128)S(6)} %copy.15.refs_1_, f32[2,50]{1,0:T(2,128)} %refs_2_.1, bf16[384,3072]{1,0:T(8,128)(2,1)} %refs_3_.1, f32[50,2,3072]{2,1,0:T(2,128)} %refs_4_.1, bf16[3,3072,384]{2,1,0:T(8,128)(2,1)} %bitcast.1, ...), custom_call_target="tpu_custom_call" | custom-call | tf_op jit(solution)/shard_map/pallas_call | solution.py:425
  40.8 0.7 %copy.12 = bf16[384,384]{1,0:T(8,128)(2,1)} copy(bf16[384,384]{1,0:T(8,128)(2,1)S(1)} %get-tuple-element.2) | data formatting | bytes 589824
  41.5 0.6 %copy.13 = bf16[6,384]{1,0:T(8,128)(2,1)} copy(bf16[6,384]{1,0:T(8,128)(2,1)S(1)} %get-tuple-element.3) | data formatting | bytes 9216
